TPU v7x, 32 devices: a whole 2x2x4 slice. The times are simulated.
32 devices in a mesh: vid: 4 (over z), ty: 2 (over y), tx: 4 (over x, core).
Axes of the slice: x: 2, y: 2, z: 4, core: 2. Of those that a mesh axis runs over, the one named last changes fastest.
Arguments:
- latent_shards: bfloat16 [4, 99328], P('vid', ('ty', 'tx')), may hold values from -6 to 6
- shard_starts: int32 [4, 9], P('vid'), may hold values from 0 to 4096, as said below
- frame_dims: int32 [4, 2], P('vid'), may hold values from 16 to 128, as said below
- latent_cache: bfloat16 [4, 2, 32, 2048], P('vid', None, 'ty', 'tx'), may hold values from -6 to 6
- feature_cache: bfloat16 [4, 2, 32, 49152], P('vid', None, 'ty', 'tx'), may hold values from -5 to 5
- in_weight: bfloat16 [432, 384], replicated, may hold values from -0.3125 to 0.3125
- in_bias: float32 [384], replicated, may hold values from -3 to 3
- norm_gain: float32 [384], replicated, may hold values from 0.1 to 1.9
- res_weight: bfloat16 [10368, 384], replicated, may hold values from -0.0625 to 0.0625
- res_bias: float32 [384], replicated, may hold values from -3 to 3
- up_weight: bfloat16 [3456, 192], replicated, may hold values from -0.109375 to 0.109375
- up_bias: float32 [192], replicated, may hold values from -3 to 3
Outputs:
- decoded: bfloat16 [4, 64, 49152], P('vid', 'ty', 'tx')
Inputs may be any that keep to these rules, and one draw needn't show every extreme that they name: `frame_dims`: row i gives video i's height, from 16 to 32, and width, from 64 to 128; one video fills the whole canvas and another is exactly 16 by 64. `shard_starts`: row i starts at 0, never falls, ends at video i's height times width, and every shard's token count fits its 776 slots; tokens lie in row-major order of the frame.
All inputs are finite; a program needn't handle non-finite values.
Results may differ from a plain program's by a relative error of at most 0.0095.
Values may be sent and summed in bfloat16 or wider, within the bound.
A program may use at most 64 MiB of HBM per device.

v0:
```python
import jax
import jax.numpy as jnp
from jax import lax
from jax.sharding import PartitionSpec as P

EPS = 1e-06


def padded_2(value, sides, width):
    for axis, dim in sides:
        size, length = (lax.axis_size(axis), value.shape[dim])
        up = [(i, (i + 1) % size) for i in range(size - 1)]
        down = [(j, i) for i, j in up]
        last = lax.slice_in_dim(value, length - width, length, axis=dim)
        leading = lax.slice_in_dim(value, 0, width, axis=dim)
        before = lax.ppermute(last, axis, up)
        after = lax.ppermute(leading, axis, down)
        value = jnp.concatenate([before, value, after], axis=dim)
    return value


def tap_sum(padded, weight, row_count, col_count):
    channels = padded.shape[-1]
    summed = jnp.zeros((row_count * col_count, weight.shape[1]), jnp.float32)
    for frame_at in range(padded.shape[0]):
        for row_at in range(3):
            for col_at in range(3):
                tap_index = (frame_at * 3 + row_at) * 3 + col_at
                window = padded[
                    frame_at, row_at : row_at + row_count, col_at : col_at + col_count
                ].reshape(row_count * col_count, channels)
                summed = summed + jnp.dot(
                    window,
                    weight[tap_index * channels : (tap_index + 1) * channels],
                    preferred_element_type=jnp.float32,
                )
    return summed


def unfold_taps(padded, row_count, col_count):
    pieces = []
    for frame_at in range(padded.shape[0]):
        for row_at in range(3):
            for col_at in range(3):
                pieces.append(
                    padded[frame_at, row_at : row_at + row_count, col_at : col_at + col_count]
                )
    joined = jnp.concatenate(pieces, axis=-1)
    return joined.reshape(row_count * col_count, joined.shape[-1])


def token_routes(first, count, breadth, slot_cap, tile_rows, tile_cols, across, shard_count):
    offset = jnp.arange(slot_cap, dtype=jnp.int32)
    position = first[..., None] + offset
    live = offset < count[..., None]
    glob_row = position // breadth
    glob_col = position % breadth
    owner = jnp.where(live, glob_row // tile_rows * across + glob_col // tile_cols, shard_count)
    place = glob_row % tile_rows * tile_cols + glob_col % tile_cols
    return (owner, place)


def per_device(
    latent_shards,
    shard_starts,
    frame_dims,
    latent_cache,
    feature_cache,
    in_weight,
    in_bias,
    norm_gain,
    res_weight,
    res_bias,
    up_weight,
    up_bias,
):
    channels = in_bias.shape[0]
    latent_width = in_weight.shape[0] // 27
    out_width = up_bias.shape[0]
    tile_rows = feature_cache.shape[2]
    tile_cols = feature_cache.shape[3] // channels
    tile_cells = tile_rows * tile_cols
    across = lax.axis_size("tx")
    down_count = lax.axis_size("ty")
    shard_count = down_count * across
    row_index = lax.axis_index("ty")
    col_index = lax.axis_index("tx")
    myself = row_index * across + col_index
    height = frame_dims[0, 0]
    breadth = frame_dims[0, 1]
    starts = shard_starts[0]
    slot_cap = latent_shards.shape[1] // latent_width
    everything = lax.all_gather(latent_shards, ("ty", "tx"), axis=1, tiled=True).reshape(
        shard_count * slot_cap, latent_width
    )
    owner, place = token_routes(
        starts[:-1],
        starts[1:] - starts[:-1],
        breadth,
        slot_cap,
        tile_rows,
        tile_cols,
        across,
        shard_count,
    )
    target = jnp.where(owner == myself, place, tile_cells).reshape(-1)
    current = (
        jnp.zeros((tile_cells, latent_width), jnp.bfloat16).at[target].set(everything, mode="drop")
    )
    ycoord = row_index * tile_rows + jnp.arange(tile_rows, dtype=jnp.int32)
    xcoord = col_index * tile_cols + jnp.arange(tile_cols, dtype=jnp.int32)
    keep = ((ycoord[:, None] < height) & (xcoord[None, :] < breadth)).astype(jnp.float32)
    keep_low = keep.astype(jnp.bfloat16)[None, :, :, None]
    keep_flat = keep.reshape(-1, 1)
    lat_stack = (
        jnp.concatenate(
            [
                latent_cache[0].reshape(2, tile_rows, tile_cols, latent_width),
                current.reshape(1, tile_rows, tile_cols, latent_width),
            ],
            0,
        )
        * keep_low
    )
    lat_padded = padded_2(lat_stack, (("ty", 1), ("tx", 2)), 1)
    unfolded = unfold_taps(lat_padded, tile_rows, tile_cols)
    first_out = (jnp.dot(unfolded, in_weight, preferred_element_type=jnp.float32) + in_bias).astype(
        jnp.bfloat16
    )
    values = first_out.astype(jnp.float32)
    power = jnp.mean(values * values, axis=1, keepdims=True)
    normed = values * lax.rsqrt(power + EPS) * norm_gain
    hidden = (jax.nn.silu(normed) * keep_flat).astype(jnp.bfloat16)
    feat_stack = jnp.concatenate(
        [
            feature_cache[0].reshape(2, tile_rows, tile_cols, channels) * keep_low,
            hidden.reshape(1, tile_rows, tile_cols, channels),
        ],
        0,
    )
    feat_padded = padded_2(feat_stack, (("ty", 1), ("tx", 2)), 1)
    branch = tap_sum(feat_padded, res_weight, tile_rows, tile_cols)
    mixed = (
        ((values + branch + res_bias) * keep_flat)
        .astype(jnp.bfloat16)
        .reshape(tile_rows, tile_cols, channels)
    )
    low_padded = padded_2(mixed, (("ty", 0), ("tx", 1)), 1)
    grown_padded = jnp.repeat(jnp.repeat(low_padded, 2, axis=0), 2, axis=1)[1:-1, 1:-1]
    result = tap_sum(grown_padded[None], up_weight, 2 * tile_rows, 2 * tile_cols) + up_bias
    keep_high = jnp.repeat(jnp.repeat(keep, 2, axis=0), 2, axis=1).reshape(-1, 1)
    return (
        (result * keep_high)
        .astype(jnp.bfloat16)
        .reshape(1, 2 * tile_rows, 2 * tile_cols * out_width)
    )


def solution(mesh):
    return jax.shard_map(
        per_device,
        mesh=mesh,
        in_specs=(
            P("vid", ("ty", "tx")),
            P("vid", None),
            P("vid", None),
            P("vid", None, "ty", "tx"),
            P("vid", None, "ty", "tx"),
            P(),
            P(),
            P(),
            P(),
            P(),
            P(),
            P(),
        ),
        out_specs=P("vid", "ty", "tx"),
        check_vma=False,
    )
```

profile of v0, /device:TPU:1, one launch (start us, length us, event | category | flops | bytes accessed | tf_op | source)
XLA Modules:
  0.0 160.1 jit_solution(8422800603614920463)
XLA Ops:
  0.0 0.7 slice_bitcast_fusion.3
  0.7 0.8 bitcast_subtract_fusion
  1.5 1.3 fusion.105
  4.7 1.3 fusion.94
  6.2 1.0 fusion.95
  7.5 11.2 %all_gather.3 = bf16[1,99328]{1,0:T(2,128)(2,1)S(1)} all-gather(bf16[1,12416]{1,0:T(2,128)(2,1)} %param.12), channel_id=1, replica_groups=mesh['vid'=4,'ty'=2,'tx'=4] {'ty','tx'}, dimensions={1}, use_global_device_ids=true | all-gather | bytes 223488 | tf_op jit(solution)/shard_map/all_gather | solution.py:93
  18.7 1.2 reduce.1
  20.0 1.0 reshape.439
  21.0 0.6 add_compare_fusion
  21.8 0.7 add_compare_fusion.1
  23.1 24.5 %scatter_custom_fusion = bf16[512,16]{1,0:T(8,128)(2,1)S(1)} fusion(s32[6208]{0:T(1024)S(1)} %fusion.97, bf16[6208,16]{1,0:T(8,128)(2,1)S(1)} %reshape.439, bf16[]{:T(256)} %constant.70.clone.1), kind=kCustom, calls=%fused_computation.159 | custom fusion | bytes 16386 | tf_op jit(solution)/shard_map/scatter | solution.py:108
  47.8 2.9 %collective-permute-start = (bf16[3,1,32,16]{3,2,1,0:T(8,128)(2,1)S(1)}, bf16[3,1,32,16]{3,2,1,0:T(8,128)(2,1)S(1)}, u32[]{:S(2)}, u32[]{:S(2)}) collective-permute-start(bf16[3,1,32,16]{3,2,1,0:T(8,128)(2,1)S(1)} %get-tuple-element.84), channel_id=1, source_target_pairs={{0,4},{1,5},{2,6},{3,7},{8,12},{9,13},{10,14},{11,15},{16,20},{17,... | collective-permute-start | bytes 9224 | tf_op jit(solution)/shard_map/ppermute | solution.py:16
  50.6 1.3 collective-permute-start.1
  52.3 1.4 fusion.72
  53.7 1.5 collective-permute-done.1
  55.3 0.7 fusion.103
  56.2 3.5 %collective-permute-start.3 = (bf16[3,18,1,16]{3,2,1,0:T(2,128)(2,1)}, bf16[3,18,1,16]{3,2,1,0:T(2,128)(2,1)}, u32[]{:S(2)}, u32[]{:S(2)}) collective-permute-start(bf16[3,18,1,16]{3,2,1,0:T(2,128)(2,1)} %get-tuple-element.68), channel_id=1, source_target_pairs={{1,0},{2,1},{3,2},{5,4},{6,5},{7,6},{9,8},{10,9},{11,10},{13,12},{... | collective-permute-start | bytes 5192 | tf_op jit(solution)/shard_map/ppermute | solution.py:17
  59.7 2.5 %collective-permute-start.2 = (bf16[3,18,1,16]{3,2,1,0:T(2,128)(2,1)}, bf16[3,18,1,16]{3,2,1,0:T(2,128)(2,1)}, u32[]{:S(2)}, u32[]{:S(2)}) collective-permute-start(bf16[3,18,1,16]{3,2,1,0:T(2,128)(2,1)} %get-tuple-element.69), channel_id=1, source_target_pairs={{0,1},{1,2},{2,3},{4,5},{5,6},{6,7},{8,9},{9,10},{10,11},{12,13},{... | collective-permute-start | bytes 5192 | tf_op jit(solution)/shard_map/ppermute | solution.py:16
  62.2 0.8 pad_maximum_fusion.11
  63.0 1.6 copy.41
  64.5 1.0 copy.42
  66.1 1.2 copy.23
  67.7 0.7 concatenate.149
  68.4 1.2 copy.19
  70.0 0.6 constant_dynamic-update-slice_fusion.26
  72.9 0.6 constant_dynamic-update-slice_fusion.25
  73.5 0.6 constant_dynamic-update-slice_fusion.24
  74.1 0.6 constant_dynamic-update-slice_fusion.23
  74.7 0.6 constant_dynamic-update-slice_fusion.22
  75.4 0.6 constant_dynamic-update-slice_fusion.21
  88.7 1.7 %multiply_reduce_fusion = (f32[512]{0:T(512)S(1)}, f32[512,384]{1,0:T(8,128)S(1)}) fusion(f32[384]{0:T(512)S(1)} %copy-done.16, bf16[512,432]{0,1:T(8,128)(2,1)} %constant_dynamic-update-slice_fusion, bf16[432,384]{1,0:T(8,128)(2,1)S(1)} %copy-done), kind=kOutput, calls=%fused_computation.50 | convolution fusion | flops 170851840 | bytes 1564160 | tf_op jit(solution)/shard_map/dot_general | solution.py:127
  90.8 2.3 %collective-permute-start.4 = (bf16[3,1,32,384]{3,2,1,0:T(8,128)(2,1)S(1)}, bf16[3,1,32,384]{3,2,1,0:T(8,128)(2,1)S(1)}, u32[]{:S(2)}, u32[]{:S(2)}) collective-permute-start(bf16[3,1,32,384]{3,2,1,0:T(8,128)(2,1)S(1)} %get-tuple-element.45), channel_id=1, source_target_pairs={{0,4},{1,5},{2,6},{3,7},{8,12},{9,13},{10,14},{11,15},{16,20},{17,... | collective-permute-start | bytes 221192 | tf_op jit(solution)/shard_map/ppermute | solution.py:16
  93.1 1.3 collective-permute-start.5
  94.4 1.4 fusion.38
  95.7 2.9 %collective-permute-done.5 = bf16[3,1,32,384]{3,2,1,0:T(8,128)(2,1)S(1)} collective-permute-done((bf16[3,1,32,384]{3,2,1,0:T(8,128)(2,1)S(1)}, bf16[3,1,32,384]{3,2,1,0:T(8,128)(2,1)S(1)}, u32[]{:S(2)}, u32[]{:S(2)}) %collective-permute-start.5) | collective-permute-done | bytes 73760 | tf_op jit(solution)/shard_map/ppermute | solution.py:17
  99.0 1.4 fusion.78
  100.5 3.3 %collective-permute-start.6 = (bf16[3,18,1,384]{3,2,1,0:T(2,128)(2,1)S(1)}, bf16[3,18,1,384]{3,2,1,0:T(2,128)(2,1)S(1)}, u32[]{:S(2)}, u32[]{:S(2)}) collective-permute-start(bf16[3,18,1,384]{3,2,1,0:T(2,128)(2,1)S(1)} %get-tuple-element.34), channel_id=1, source_target_pairs={{0,1},{1,2},{2,3},{4,5},{5,6},{6,7},{8,9},{9,10},{10,11},{12,13},{... | collective-permute-start | bytes 124424 | tf_op jit(solution)/shard_map/ppermute | solution.py:16
  103.8 2.1 %collective-permute-start.7 = (bf16[3,18,1,384]{3,2,1,0:T(2,128)(2,1)S(1)}, bf16[3,18,1,384]{3,2,1,0:T(2,128)(2,1)S(1)}, u32[]{:S(2)}, u32[]{:S(2)}) collective-permute-start(bf16[3,18,1,384]{3,2,1,0:T(2,128)(2,1)S(1)} %get-tuple-element.35), channel_id=1, source_target_pairs={{1,0},{2,1},{3,2},{5,4},{6,5},{7,6},{9,8},{10,9},{11,10},{13,12},{... | collective-permute-start | bytes 124424 | tf_op jit(solution)/shard_map/ppermute | solution.py:17
  106.0 1.4 fusion.55
  109.0 1.3 fusion.33
  110.3 1.9 %maximum_maximum_fusion = (bf16[3,18,33,384]{3,2,1,0:T(8,128)(2,1)S(1)}, bf16[3,18,33,384]{3,2,1,0:T(8,128)(2,1)S(1)}) fusion(bf16[3,1,32,384]{3,2,1,0:T(8,128)(2,1)S(1)} %collective-permute-done.5, bf16[1,16,32,384]{3,2,1,0:T(8,128)(2,1)S(1)} %bitcast.185, bf16[2,16,32,384]{3,2,1,0:T(8,128)(2,1)S(1)} %bitcast_multiply_fusion, ...), kind=kLoop, calls=%fused_computation.13 | loop fusion | flops 13685760 | bytes 4147200 | tf_op jit(solution)/shard_map/concatenate | solution.py:18
  112.2 2.0 %fusion.101 = (bf16[1,16,32,384]{3,2,1,0:T(8,128)(2,1)}, bf16[1,16,32,384]{3,2,1,0:T(8,128)(2,1)}, bf16[1,16,32,384]{3,2,1,0:T(8,128)(2,1)S(1)}, bf16[1,16,32,38...) fusion(bf16[3,18,33,384]{3,2,1,0:T(8,128)(2,1)S(1)} %get-tuple-, ...), kind=kLoop, calls=%fused_computation.218 | loop fusion | bytes 14155776 | tf_op jit(solution)/shard_map/slice | solution.py:29
  120.7 0.8 fusion.13
  121.5 0.8 fusion.21
  123.3 1.4 collective-permute-start.8
  124.8 1.3 collective-permute-start.9
  126.1 3.3 %collective-permute-done.9 = bf16[1,32,384]{2,1,0:T(8,128)(2,1)S(1)} collective-permute-done((bf16[1,32,384]{2,1,0:T(8,128)(2,1)S(1)}, bf16[1,32,384]{2,1,0:T(8,128)(2,1)S(1)}, u32[]{:S(2)}, u32[]{:S(2)}) %collective-permute-start.9) | collective-permute-done | bytes 24608 | tf_op jit(solution)/shard_map/ppermute | solution.py:17
  129.4 5.1 %collective-permute-start.10 = (bf16[18,1,384]{2,1,0:T(2,128)(2,1)S(1)}, bf16[18,1,384]{2,1,0:T(2,128)(2,1)S(1)}, u32[]{:S(2)}, u32[]{:S(2)}) collective-permute-start(bf16[18,1,384]{2,1,0:T(2,128)(2,1)S(1)} %get-tuple-element.48), channel_id=1, source_target_pairs={{0,1},{1,2},{2,3},{4,5},{5,6},{6,7},{8,9},{9,10},{10,11},{12,13},{... | collective-permute-start | bytes 41480 | tf_op jit(solution)/shard_map/ppermute | solution.py:16
  134.5 2.2 %collective-permute-start.11 = (bf16[18,1,384]{2,1,0:T(2,128)(2,1)S(1)}, bf16[18,1,384]{2,1,0:T(2,128)(2,1)S(1)}, u32[]{:S(2)}, u32[]{:S(2)}) collective-permute-start(bf16[18,1,384]{2,1,0:T(2,128)(2,1)S(1)} %get-tuple-element.49), channel_id=1, source_target_pairs={{1,0},{2,1},{3,2},{5,4},{6,5},{7,6},{9,8},{10,9},{11,10},{13,12},{... | collective-permute-start | bytes 41480 | tf_op jit(solution)/shard_map/ppermute | solution.py:17
  137.2 2.5 %collective-permute-done.11 = bf16[18,1,384]{2,1,0:T(2,128)(2,1)S(1)} collective-permute-done((bf16[18,1,384]{2,1,0:T(2,128)(2,1)S(1)}, bf16[18,1,384]{2,1,0:T(2,128)(2,1)S(1)}, u32[]{:S(2)}, u32[]{:S(2)}) %collective-permute-start.11) | collective-permute-done | bytes 13856 | tf_op jit(solution)/shard_map/ppermute | solution.py:17
  140.0 2.2 %broadcast_in_dim.42 = bf16[36,34,2,384]{3,2,1,0:T(2,128)(2,1)} broadcast(bf16[36,34,384]{2,1,0:T(8,128)(2,1)S(1)} %bitcast.197), dimensions={0,1,3} | broadcast | bytes 2820096 | tf_op jit(solution)/shard_map/broadcast_in_dim | solution.py:149
  142.2 4.2 %reshape.431 = bf16[36,68,384]{2,1,0:T(8,128)(2,1)S(1)} reshape(bf16[36,34,2,384]{3,2,1,0:T(2,128)(2,1)} %broadcast_in_dim.42) | data formatting | bytes 3760128 | tf_op jit(solution)/shard_map/reshape | solution.py:149
  146.4 0.9 slice_bitcast_fusion
  147.3 3.6 %fusion.100 = (bf16[1,32,64,384]{3,2,1,0:T(8,128)(2,1)S(1)}, bf16[1,32,64,384]{3,2,1,0:T(8,128)(2,1)S(1)}, bf16[1,32,64,384]{3,2,1,0:T(8,128)(2,1)S(1)}, bf16[1,...) fusion(bf16[1,34,66,384]{3,2,1,0:T(8,128)(2,1)S(1)} %slice_bitc, ...), kind=kLoop, calls=%fused_computation.217 | loop fusion | bytes 28311552 | tf_op jit(solution)/shard_map/slice | solution.py:29
  150.9 0.7 fusion.89
  151.6 0.7 convolution_add_fusion.7
  152.4 0.7 convolution_add_fusion.6
  153.1 0.7 convolution_add_fusion.5
  153.8 0.7 convolution_add_fusion.4
  154.6 0.7 convolution_add_fusion.3
  155.3 0.7 convolution_add_fusion.2
  156.0 0.7 convolution_add_fusion.1
  156.8 0.7 fusion.2
  158.0 2.1 %reshape.433 = bf16[1,32,12288]{2,1,0:T(8,128)(2,1)} reshape(bf16[2048,192]{1,0:T(8,128)(2,1)S(1)} %copy.50) | data formatting | bytes 1572864 | tf_op jit(solution)/shard_map/reshape | solution.py:155
  (161 shorter events, 29.8 us)
Async XLA Ops:
  0.0 88.7 %copy-start = (bf16[432,384]{1,0:T(8,128)(2,1)S(1)}, bf16[432,384]{1,0:T(8,128)(2,1)}, u32[]{:S(2)}) copy-start(bf16[432,384]{1,0:T(8,128)(2,1)} %param.17) | copy-start | bytes 995332
  0.0 21.6 %copy-start.12 = (bf16[1,2,16,512]{3,2,1,0:T(8,128)(2,1)S(1)}, bf16[1,2,16,512]{3,2,1,0:T(8,128)(2,1)}, u32[]{:S(2)}) copy-start(bf16[1,2,16,512]{3,2,1,0:T(8,128)(2,1)} %param.15) | copy-start | bytes 98308
  20.0 32.0 %copy-start.9 = (bf16[1,2,16,12288]{3,2,1,0:T(8,128)(2,1)S(1)}, bf16[1,2,16,12288]{3,2,1,0:T(8,128)(2,1)}, u32[]{:S(2)}) copy-start(bf16[1,2,16,12288]{3,2,1,0:T(8,128)(2,1)} %param.16) | copy-start | bytes 2359300
  47.8 6.0 %collective-permute-start = (bf16[3,1,32,16]{3,2,1,0:T(8,128)(2,1)S(1)}, bf16[3,1,32,16]{3,2,1,0:T(8,128)(2,1)S(1)}, u32[]{:S(2)}, u32[]{:S(2)}) collective-permute-start(bf16[3,1,32,16]{3,2,1,0:T(8,128)(2,1)S(1)} %get-tuple-element.84), channel_id=1, source_target_pairs={{0,4},{1,5},{2,6},{3,7},{8,12},{9,13},{10,14},{11,15},{16,20},{17,... | collective-permute-start | bytes 9224 | tf_op jit(solution)/shard_map/ppermute | solution.py:16
  50.6 4.6 %collective-permute-start.1 = (bf16[3,1,32,16]{3,2,1,0:T(8,128)(2,1)S(1)}, bf16[3,1,32,16]{3,2,1,0:T(8,128)(2,1)S(1)}, u32[]{:S(2)}, u32[]{:S(2)}) collective-permute-start(bf16[3,1,32,16]{3,2,1,0:T(8,128)(2,1)S(1)} %get-tuple-element.85), channel_id=1, source_target_pairs={{4,0},{5,1},{6,2},{7,3},{12,8},{13,9},{14,10},{15,11},{20,16},{21,... | collective-permute-start | bytes 9224 | tf_op jit(solution)/shard_map/ppermute | solution.py:17
  56.2 9.9 %collective-permute-start.3 = (bf16[3,18,1,16]{3,2,1,0:T(2,128)(2,1)}, bf16[3,18,1,16]{3,2,1,0:T(2,128)(2,1)}, u32[]{:S(2)}, u32[]{:S(2)}) collective-permute-start(bf16[3,18,1,16]{3,2,1,0:T(2,128)(2,1)} %get-tuple-element.68), channel_id=1, source_target_pairs={{1,0},{2,1},{3,2},{5,4},{6,5},{7,6},{9,8},{10,9},{11,10},{13,12},{... | collective-permute-start | bytes 5192 | tf_op jit(solution)/shard_map/ppermute | solution.py:17
  59.7 8.7 %collective-permute-start.2 = (bf16[3,18,1,16]{3,2,1,0:T(2,128)(2,1)}, bf16[3,18,1,16]{3,2,1,0:T(2,128)(2,1)}, u32[]{:S(2)}, u32[]{:S(2)}) collective-permute-start(bf16[3,18,1,16]{3,2,1,0:T(2,128)(2,1)} %get-tuple-element.69), channel_id=1, source_target_pairs={{0,1},{1,2},{2,3},{4,5},{5,6},{6,7},{8,9},{9,10},{10,11},{12,13},{... | collective-permute-start | bytes 5192 | tf_op jit(solution)/shard_map/ppermute | solution.py:16
  70.8 2.2 %copy-start.10 = (bf16[512,16]{0,1:T(8,128)(2,1)S(1)}, bf16[512,16]{0,1:T(8,128)(2,1)}, u32[]{:S(2)}) copy-start(bf16[512,16]{0,1:T(8,128)(2,1)} %copy.41) | copy-start | bytes 49156
  70.8 2.8 %copy-start.11 = (bf16[512,16]{0,1:T(8,128)(2,1)S(1)}, bf16[512,16]{0,1:T(8,128)(2,1)}, u32[]{:S(2)}) copy-start(bf16[512,16]{0,1:T(8,128)(2,1)} %concatenate.149) | copy-start | bytes 49156
  71.3 17.4 %copy-start.16 = (f32[384]{0:T(512)S(1)}, f32[384]{0:T(512)}, u32[]{:S(2)}) copy-start(f32[384]{0:T(512)} %param.18) | copy-start | bytes 4612
  72.6 17.8 %copy-start.13 = (f32[384]{0:T(512)S(1)}, f32[384]{0:T(512)}, u32[]{:S(2)}) copy-start(f32[384]{0:T(512)} %param.19) | copy-start | bytes 4612
  88.7 18.6 %slice-start = ((s8[7962624]{0:T(1024)(128)(4,1)}), s8[4194304]{0:T(1024)(128)(4,1)S(1)}, s32[]{:S(2)}) async-start(s8[7962624]{0:T(1024)(128)(4,1)} %bitcast.186), calls=%async_computation | async-start | bytes 8388608
  90.8 4.9 %collective-permute-start.4 = (bf16[3,1,32,384]{3,2,1,0:T(8,128)(2,1)S(1)}, bf16[3,1,32,384]{3,2,1,0:T(8,128)(2,1)S(1)}, u32[]{:S(2)}, u32[]{:S(2)}) collective-permute-start(bf16[3,1,32,384]{3,2,1,0:T(8,128)(2,1)S(1)} %get-tuple-element.45), channel_id=1, source_target_pairs={{0,4},{1,5},{2,6},{3,7},{8,12},{9,13},{10,14},{11,15},{16,20},{17,... | collective-permute-start | bytes 221192 | tf_op jit(solution)/shard_map/ppermute | solution.py:16
  93.1 5.6 %collective-permute-start.5 = (bf16[3,1,32,384]{3,2,1,0:T(8,128)(2,1)S(1)}, bf16[3,1,32,384]{3,2,1,0:T(8,128)(2,1)S(1)}, u32[]{:S(2)}, u32[]{:S(2)}) collective-permute-start(bf16[3,1,32,384]{3,2,1,0:T(8,128)(2,1)S(1)} %get-tuple-element.46), channel_id=1, source_target_pairs={{4,0},{5,1},{6,2},{7,3},{12,8},{13,9},{14,10},{15,11},{20,16},{21,... | collective-permute-start | bytes 221192 | tf_op jit(solution)/shard_map/ppermute | solution.py:17
  95.7 11.6 %slice-start.1 = ((s8[7962624]{0:T(1024)(128)(4,1)}), s8[3768320]{0:T(1024)(128)(4,1)S(1)}, s32[]{:S(2)}) async-start(s8[7962624]{0:T(1024)(128)(4,1)} %bitcast.186), calls=%async_computation.1 | async-start | bytes 7536640
  100.5 9.7 %collective-permute-start.6 = (bf16[3,18,1,384]{3,2,1,0:T(2,128)(2,1)S(1)}, bf16[3,18,1,384]{3,2,1,0:T(2,128)(2,1)S(1)}, u32[]{:S(2)}, u32[]{:S(2)}) collective-permute-start(bf16[3,18,1,384]{3,2,1,0:T(2,128)(2,1)S(1)} %get-tuple-element.34), channel_id=1, source_target_pairs={{0,1},{1,2},{2,3},{4,5},{5,6},{6,7},{8,9},{9,10},{10,11},{12,13},{... | collective-permute-start | bytes 124424 | tf_op jit(solution)/shard_map/ppermute | solution.py:16
  103.8 6.4 %collective-permute-start.7 = (bf16[3,18,1,384]{3,2,1,0:T(2,128)(2,1)S(1)}, bf16[3,18,1,384]{3,2,1,0:T(2,128)(2,1)S(1)}, u32[]{:S(2)}, u32[]{:S(2)}) collective-permute-start(bf16[3,18,1,384]{3,2,1,0:T(2,128)(2,1)S(1)} %get-tuple-element.35), channel_id=1, source_target_pairs={{1,0},{2,1},{3,2},{5,4},{6,5},{7,6},{9,8},{10,9},{11,10},{13,12},{... | collective-permute-start | bytes 124424 | tf_op jit(solution)/shard_map/ppermute | solution.py:17
  117.8 1.0 copy-start.7
  118.2 1.0 copy-start.6
  118.6 1.1 copy-start.5
  119.2 1.0 copy-start.4
  121.5 1.1 copy-start.2
  121.5 1.2 copy-start.3
  121.5 1.2 copy-start.14
  123.3 2.7 %collective-permute-start.8 = (bf16[1,32,384]{2,1,0:T(8,128)(2,1)S(1)}, bf16[1,32,384]{2,1,0:T(8,128)(2,1)S(1)}, u32[]{:S(2)}, u32[]{:S(2)}) collective-permute-start(bf16[1,32,384]{2,1,0:T(8,128)(2,1)S(1)} %get-tuple-element.76), channel_id=1, source_target_pairs={{0,4},{1,5},{2,6},{3,7},{8,12},{9,13},{10,14},{11,15},{16,20},{17,... | collective-permute-start | bytes 73736 | tf_op jit(solution)/shard_map/ppermute | solution.py:16
  124.8 4.6 %collective-permute-start.9 = (bf16[1,32,384]{2,1,0:T(8,128)(2,1)S(1)}, bf16[1,32,384]{2,1,0:T(8,128)(2,1)S(1)}, u32[]{:S(2)}, u32[]{:S(2)}) collective-permute-start(bf16[1,32,384]{2,1,0:T(8,128)(2,1)S(1)} %get-tuple-element.77), channel_id=1, source_target_pairs={{4,0},{5,1},{6,2},{7,3},{12,8},{13,9},{14,10},{15,11},{20,16},{21,... | collective-permute-start | bytes 73736 | tf_op jit(solution)/shard_map/ppermute | solution.py:17
  129.4 7.8 %collective-permute-start.10 = (bf16[18,1,384]{2,1,0:T(2,128)(2,1)S(1)}, bf16[18,1,384]{2,1,0:T(2,128)(2,1)S(1)}, u32[]{:S(2)}, u32[]{:S(2)}) collective-permute-start(bf16[18,1,384]{2,1,0:T(2,128)(2,1)S(1)} %get-tuple-element.48), channel_id=1, source_target_pairs={{0,1},{1,2},{2,3},{4,5},{5,6},{6,7},{8,9},{9,10},{10,11},{12,13},{... | collective-permute-start | bytes 41480 | tf_op jit(solution)/shard_map/ppermute | solution.py:16
  134.5 5.2 %collective-permute-start.11 = (bf16[18,1,384]{2,1,0:T(2,128)(2,1)S(1)}, bf16[18,1,384]{2,1,0:T(2,128)(2,1)S(1)}, u32[]{:S(2)}, u32[]{:S(2)}) collective-permute-start(bf16[18,1,384]{2,1,0:T(2,128)(2,1)S(1)} %get-tuple-element.49), channel_id=1, source_target_pairs={{1,0},{2,1},{3,2},{5,4},{6,5},{7,6},{9,8},{10,9},{11,10},{13,12},{... | collective-permute-start | bytes 41480 | tf_op jit(solution)/shard_map/ppermute | solution.py:17
  147.3 3.6 %copy-start.8 = (bf16[3456,192]{0,1:T(8,128)(2,1)S(1)}, bf16[3456,192]{0,1:T(8,128)(2,1)}, u32[]{:S(2)}) copy-start(bf16[3456,192]{0,1:T(8,128)(2,1)} %param.22) | copy-start | bytes 3981316
  156.0 0.7 copy-start.15
  156.8 3.3 %copy-start.1 = (bf16[432,384]{1,0:T(8,128)(2,1)S(1)}, bf16[432,384]{1,0:T(8,128)(2,1)}, u32[]{:S(2)}) copy-start(bf16[432,384]{1,0:T(8,128)(2,1)} %param.17) | copy-start | bytes 995332
where the time goes:
time: 161 us; the launch traced here: 160 us
  local copies, waits for them, and re-layouts  71.1 us (44%)
  starting transfers between devices  29.1 us (18%)
  matrix products  24.5 us (15%)
  blocking collectives  11.2 us (7%)
  other arithmetic  11.1 us (7%)
  waiting for transfers between devices  10.2 us (6%)
  between operations  2.86 us (2%)
    scatter x1, local copies, waits for them, and re-layouts, per_device(): jnp.zeros((tile_cells, latent_width), jnp.bfloat16).at[target]  24.5 us
    dot_general x36, matrix products, tap_sum(): jnp.dot(window, weight[tap_index * channels:(tap_index + 1) * channels],...  22.8 us
    ppermute x6, starting transfers between devices, padded_2(): before = lax.ppermute(last, axis, up)  17.4 us
    unnamed x65, local copies, waits for them, and re-layouts  16.8 us
    ppermute x6, starting transfers between devices, padded_2(): after = lax.ppermute(leading, axis, down)  11.7 us
    all_gather x1, blocking collectives, per_device(): lax.all_gather(latent_shards, ('ty', 'tx'), axis=1, tiled=True)  11.2 us
    ppermute x6, waiting for transfers between devices, padded_2(): after = lax.ppermute(leading, axis, down)  10.2 us
    concatenate x28, local copies, waits for them, and re-layouts, unfold_taps(): joined = jnp.concatenate(pieces, axis=-1)  6.48 us
  transfers between devices with their start and end apart: 12, of which 4 were waited for; matrix products, arithmetic and copies ran while one was open for 9% of the time, Pallas kernels for 0%

commit v1 on v0

--- a/solution.py
+++ b/solution.py
@@ -4,6 +4,28 @@
 from jax.sharding import PartitionSpec as P
 
 EPS = 1e-06
+
+
+def in_order(pieces, dim):
+    shape = list(pieces.shape[1:])
+    shape[dim] *= pieces.shape[0]
+    return jnp.moveaxis(pieces, 0, dim).reshape(shape)
+
+
+def collect(x, axis, dim):
+    count = lax.axis_size(axis)
+    pairs = [(i, (i + 1) % count) for i in range(count)]
+    back = [(b, a) for a, b in pairs]
+    lower, upper = ([], [])
+    for step in range(count - 1):
+        if step % 2 == 0:
+            lower.append(lax.ppermute(lower[-1] if lower else x, axis, pairs))
+        else:
+            upper.append(lax.ppermute(upper[-1] if upper else x, axis, back))
+    tiles = jnp.stack([*lower[::-1], x, *upper])
+    shift = lax.axis_index(axis) - len(lower)
+    tiles = tiles[(jnp.arange(count) - shift) % count]
+    return in_order(tiles, dim)
 
 
 def padded_2(value, sides, width):
@@ -90,7 +112,7 @@
     breadth = frame_dims[0, 1]
     starts = shard_starts[0]
     slot_cap = latent_shards.shape[1] // latent_width
-    everything = lax.all_gather(latent_shards, ("ty", "tx"), axis=1, tiled=True).reshape(
+    everything = collect(latent_shards, ("ty", "tx"), 1).reshape(
         shard_count * slot_cap, latent_width
     )
     owner, place = token_routes(

time: 161 us -> 172 us (1.068)
  blocking collectives: 11.2 us -> 0 us
  starting transfers between devices: 29.1 us -> 40.2 us
  local copies, waits for them, and re-layouts: 71.1 us -> 79.1 us
  waiting for transfers between devices: 10.2 us -> 13.5 us
    all_gather x1 -> x0, blocking collectives: 11.2 us -> none  [per_device(): lax.all_gather(latent_shards, ('ty', 'tx'), axis=1, tiled=True)]
    ppermute x0 -> x7, starting transfers between devices: none -> 9.13 us  [the longest x4 9.07 us: collect(): lower.append(lax.ppermute(lower[-1] if lower else x, axis, pairs))]
    ppermute x6, starting transfers between devices: 11.7 us -> 16.8 us  [padded_2(): after = lax.ppermute(leading, axis, down)]
    another operation x0 -> x2, local copies, waits for them, and re-layouts: none -> 3.8 us  [the longest x1 2.09 us: per_device(): collect(latent_shards, ('ty', 'tx'), 1)]
    ppermute x6, starting transfers between devices: 17.4 us -> 14.2 us  [padded_2(): before = lax.ppermute(last, axis, up)]
    ppermute x0 -> x7, waiting for transfers between devices: none -> 3.07 us  [the longest x4 1.87 us: collect(): lower.append(lax.ppermute(lower[-1] if lower else x, axis, pairs))]
    concatenate x28, local copies, waits for them, and re-layouts: 6.48 us -> 8.59 us  [unfold_taps(): joined = jnp.concatenate(pieces, axis=-1)]
    unnamed x65 -> x77, local copies, waits for them, and re-layouts: 16.8 us -> 18.4 us
  transfers between devices with their start and end apart: 12 -> 19, of which waited for: 4 -> 9; matrix products, arithmetic and copies ran while one was open for 9% -> 15% of each run, Pallas kernels for 0% -> 0%
where the time goes in v1:
time: 172 us; the launch traced here: 171 us
  local copies, waits for them, and re-layouts  79.1 us (46%)
  starting transfers between devices  40.2 us (23%)
  matrix products  24.5 us (14%)
  waiting for transfers between devices  13.5 us (8%)
  other arithmetic  10.6 us (6%)
  between operations  2.88 us (2%)
    scatter x1, local copies, waits for them, and re-layouts, per_device(): jnp.zeros((tile_cells, latent_width), jnp.bfloat16).at[target]  24.5 us
    dot_general x36, matrix products, tap_sum(): jnp.dot(window, weight[tap_index * channels:(tap_index + 1) * channels],...  22.8 us
    unnamed x77, local copies, waits for them, and re-layouts  18.4 us
    ppermute x6, starting transfers between devices, padded_2(): after = lax.ppermute(leading, axis, down)  16.8 us
    ppermute x6, starting transfers between devices, padded_2(): before = lax.ppermute(last, axis, up)  14.2 us
    ppermute x6, waiting for transfers between devices, padded_2(): after = lax.ppermute(leading, axis, down)  10.4 us
    ppermute x4, starting transfers between devices, collect(): lower.append(lax.ppermute(lower[-1] if lower else x, axis, pairs))  9.07 us
    concatenate x28, local copies, waits for them, and re-layouts, unfold_taps(): joined = jnp.concatenate(pieces, axis=-1)  8.59 us
  transfers between devices with their start and end apart: 19, of which 9 were waited for; matrix products, arithmetic and copies ran while one was open for 15% of the time, Pallas kernels for 0%

profile of v1, /device:TPU:1, one launch (start us, length us, event | category | flops | bytes accessed | tf_op | source)
XLA Modules:
  0.0 170.8 jit_solution(2395818327588983249)
XLA Ops:
  0.0 2.6 %collective-permute-start = (bf16[1,12416]{1,0:T(2,128)(2,1)}, bf16[1,12416]{1,0:T(2,128)(2,1)S(1)}, u32[]{:S(2)}, u32[]{:S(2)}) collective-permute-start(bf16[1,12416]{1,0:T(2,128)(2,1)} %param.12), channel_id=1, source_target_pairs={{0,1},{1,2},{2,3},{3,4},{4,5},{5,6},{6,7},{7,0},{8,9},{9,10},{10,1... | collective-permute-start | bytes 74504 | tf_op jit(solution)/shard_map/ppermute | solution.py:22
  2.6 0.7 slice_bitcast_fusion.3
  3.3 0.8 bitcast_subtract_fusion
  4.1 1.3 fusion.107
  7.2 1.2 fusion.94
  8.5 1.0 fusion.95
  10.1 1.2 copy.51
  11.4 0.7 add_compare_fusion.1
  12.8 1.8 %collective-permute-start.1 = (bf16[1,12416]{1,0:T(2,128)(2,1)S(1)}, bf16[1,12416]{1,0:T(2,128)(2,1)S(1)}, u32[]{:S(2)}, u32[]{:S(2)}) collective-permute-start(bf16[1,12416]{1,0:T(2,128)(2,1)S(1)} %collective-permute-done), channel_id=1, source_target_pairs={{0,1},{1,2},{2,3},{3,4},{4,5},{5,6},{6,7},{7,0},{8,9},{9,10},{10,1... | collective-permute-start | bytes 74504 | tf_op jit(solution)/shard_map/ppermute | solution.py:22
  15.8 2.3 %collective-permute-start.2 = (bf16[1,12416]{1,0:T(2,128)(2,1)S(1)}, bf16[1,12416]{1,0:T(2,128)(2,1)S(1)}, u32[]{:S(2)}, u32[]{:S(2)}) collective-permute-start(bf16[1,12416]{1,0:T(2,128)(2,1)S(1)} %collective-permute-done.1), channel_id=1, source_target_pairs={{0,1},{1,2},{2,3},{3,4},{4,5},{5,6},{6,7},{7,0},{8,9},{9,10},{10,1... | collective-permute-start | bytes 74504 | tf_op jit(solution)/shard_map/ppermute | solution.py:22
  19.3 2.3 %collective-permute-start.3 = (bf16[1,12416]{1,0:T(2,128)(2,1)S(1)}, bf16[1,12416]{1,0:T(2,128)(2,1)S(1)}, u32[]{:S(2)}, u32[]{:S(2)}) collective-permute-start(bf16[1,12416]{1,0:T(2,128)(2,1)S(1)} %collective-permute-done.2), channel_id=1, source_target_pairs={{0,1},{1,2},{2,3},{3,4},{4,5},{5,6},{6,7},{7,0},{8,9},{9,10},{10,1... | collective-permute-start | bytes 74504 | tf_op jit(solution)/shard_map/ppermute | solution.py:22
  22.6 0.7 collective-permute-done.3
  23.3 1.7 %stack.35 = bf16[8,1,12416]{2,0,1:T(8,128)(2,1)S(1)} concatenate(bf16[1,1,12416]{2,0,1:T(2,128)(2,1)S(1)} %bitcast.258, bf16[1,1,12416]{2,0,1:T(2,128)(2,1)S(1)} %bitcast.256, bf16[1,1,12416]{2,0,1:T(2,128)(2,1)S(1)} %bitcast.254, bf16[1,1,12416]{2,0,1:T(2,128)(2,1)S(1)} %bitcast.252, bf16[1,1,12416]{2,0,1:T(2,128)(2,1)S(1)} %bitcast.251, bf16[1,1,12416]{2,0,1:T(2,128)(2,1)S(1)} %bitcast.253, ...), dimensions={0} | concatenate | bytes 397312 | tf_op jit(solution)/shard_map/stack | solution.py:25
  25.0 1.4 gather_fusion
  26.4 2.1 %reshape.494 = bf16[6208,16]{1,0:T(8,128)(2,1)S(1)} reshape(bf16[8,12416]{1,0:T(8,128)(2,1)} %gather_fusion) | data formatting | bytes 397312 | tf_op jit(solution)/shard_map/reshape;reshape;transpose | solution.py:115
  28.5 24.5 %scatter_custom_fusion = bf16[512,16]{1,0:T(8,128)(2,1)S(1)} fusion(s32[6208]{0:T(1024)S(1)} %fusion.97, bf16[6208,16]{1,0:T(8,128)(2,1)S(1)} %reshape.494, bf16[]{:T(256)} %constant.84.clone.1), kind=kCustom, calls=%fused_computation.160 | custom fusion | bytes 16386 | tf_op jit(solution)/shard_map/scatter | solution.py:130
  53.1 4.0 %collective-permute-start.7 = (bf16[3,1,32,16]{3,2,1,0:T(8,128)(2,1)S(1)}, bf16[3,1,32,16]{3,2,1,0:T(8,128)(2,1)S(1)}, u32[]{:S(2)}, u32[]{:S(2)}) collective-permute-start(bf16[3,1,32,16]{3,2,1,0:T(8,128)(2,1)S(1)} %get-tuple-element.84), channel_id=1, source_target_pairs={{0,4},{1,5},{2,6},{3,7},{8,12},{9,13},{10,14},{11,15},{16,20},{17,... | collective-permute-start | bytes 9224 | tf_op jit(solution)/shard_map/ppermute | solution.py:38
  57.2 1.3 collective-permute-start.8
  58.5 1.4 fusion.72
  59.9 1.8 %collective-permute-done.8 = bf16[3,1,32,16]{3,2,1,0:T(8,128)(2,1)S(1)} collective-permute-done((bf16[3,1,32,16]{3,2,1,0:T(8,128)(2,1)S(1)}, bf16[3,1,32,16]{3,2,1,0:T(8,128)(2,1)S(1)}, u32[]{:S(2)}, u32[]{:S(2)}) %collective-permute-start.8) | collective-permute-done | bytes 3104 | tf_op jit(solution)/shard_map/ppermute | solution.py:39
  61.9 0.7 fusion.105
  62.5 7.0 %collective-permute-start.10 = (bf16[3,18,1,16]{3,2,1,0:T(2,128)(2,1)}, bf16[3,18,1,16]{3,2,1,0:T(2,128)(2,1)}, u32[]{:S(2)}, u32[]{:S(2)}) collective-permute-start(bf16[3,18,1,16]{3,2,1,0:T(2,128)(2,1)} %get-tuple-element.68), channel_id=1, source_target_pairs={{1,0},{2,1},{3,2},{5,4},{6,5},{7,6},{9,8},{10,9},{11,10},{13,12},{... | collective-permute-start | bytes 5192 | tf_op jit(solution)/shard_map/ppermute | solution.py:39
  69.5 1.5 pad_maximum_fusion.11
  71.3 1.6 copy.41
  72.9 2.1 %collective-permute-start.9 = (bf16[3,18,1,16]{3,2,1,0:T(2,128)(2,1)}, bf16[3,18,1,16]{3,2,1,0:T(2,128)(2,1)}, u32[]{:S(2)}, u32[]{:S(2)}) collective-permute-start(bf16[3,18,1,16]{3,2,1,0:T(2,128)(2,1)} %get-tuple-element.69), channel_id=1, source_target_pairs={{0,1},{1,2},{2,3},{4,5},{5,6},{6,7},{8,9},{9,10},{10,11},{12,13},{... | collective-permute-start | bytes 5192 | tf_op jit(solution)/shard_map/ppermute | solution.py:38
  75.0 1.6 copy.42
  76.6 1.6 copy.43
  78.7 1.2 copy.23
  80.3 0.7 concatenate.149
  81.0 1.2 copy.19
  101.3 1.7 %multiply_reduce_fusion = (f32[512]{0:T(512)S(1)}, f32[512,384]{1,0:T(8,128)S(1)}) fusion(f32[384]{0:T(512)S(1)} %copy-done.22, bf16[512,432]{0,1:T(8,128)(2,1)} %constant_dynamic-update-slice_fusion, bf16[432,384]{1,0:T(8,128)(2,1)S(1)} %copy-done), kind=kOutput, calls=%fused_computation.51 | convolution fusion | flops 170851840 | bytes 1564160 | tf_op jit(solution)/shard_map/dot_general | solution.py:149
  103.4 1.3 collective-permute-start.11
  104.7 1.3 collective-permute-start.12
  106.0 1.4 fusion.38
  107.4 2.4 %collective-permute-done.12 = bf16[3,1,32,384]{3,2,1,0:T(8,128)(2,1)S(1)} collective-permute-done((bf16[3,1,32,384]{3,2,1,0:T(8,128)(2,1)S(1)}, bf16[3,1,32,384]{3,2,1,0:T(8,128)(2,1)S(1)}, u32[]{:S(2)}, u32[]{:S(2)}) %collective-permute-start.12) | collective-permute-done | bytes 73760 | tf_op jit(solution)/shard_map/ppermute | solution.py:39
  110.2 1.4 fusion.78
  111.7 2.0 %collective-permute-start.13 = (bf16[3,18,1,384]{3,2,1,0:T(2,128)(2,1)S(1)}, bf16[3,18,1,384]{3,2,1,0:T(2,128)(2,1)S(1)}, u32[]{:S(2)}, u32[]{:S(2)}) collective-permute-start(bf16[3,18,1,384]{3,2,1,0:T(2,128)(2,1)S(1)} %get-tuple-element.34), channel_id=1, source_target_pairs={{0,1},{1,2},{2,3},{4,5},{5,6},{6,7},{8,9},{9,10},{10,11},{12,13},{... | collective-permute-start | bytes 124424 | tf_op jit(solution)/shard_map/ppermute | solution.py:38
  113.7 3.8 %collective-permute-start.14 = (bf16[3,18,1,384]{3,2,1,0:T(2,128)(2,1)S(1)}, bf16[3,18,1,384]{3,2,1,0:T(2,128)(2,1)S(1)}, u32[]{:S(2)}, u32[]{:S(2)}) collective-permute-start(bf16[3,18,1,384]{3,2,1,0:T(2,128)(2,1)S(1)} %get-tuple-element.35), channel_id=1, source_target_pairs={{1,0},{2,1},{3,2},{5,4},{6,5},{7,6},{9,8},{10,9},{11,10},{13,12},{... | collective-permute-start | bytes 124424 | tf_op jit(solution)/shard_map/ppermute | solution.py:39
  117.5 1.4 fusion.55
  120.5 1.3 fusion.33
  121.7 1.9 %maximum_maximum_fusion = (bf16[3,18,33,384]{3,2,1,0:T(8,128)(2,1)S(1)}, bf16[3,18,33,384]{3,2,1,0:T(8,128)(2,1)S(1)}) fusion(bf16[3,1,32,384]{3,2,1,0:T(8,128)(2,1)S(1)} %collective-permute-done.12, bf16[1,16,32,384]{3,2,1,0:T(8,128)(2,1)S(1)} %bitcast.197, bf16[2,16,32,384]{3,2,1,0:T(8,128)(2,1)S(1)} %bitcast_multiply_fusion, ...), kind=kLoop, calls=%fused_computation.14 | loop fusion | flops 13685760 | bytes 4147200 | tf_op jit(solution)/shard_map/concatenate | solution.py:40
  123.7 2.1 %fusion.103 = (bf16[1,16,32,384]{3,2,1,0:T(8,128)(2,1)}, bf16[1,16,32,384]{3,2,1,0:T(8,128)(2,1)}, bf16[1,16,32,384]{3,2,1,0:T(8,128)(2,1)S(1)}, bf16[1,16,32,38...) fusion(bf16[3,18,33,384]{3,2,1,0:T(8,128)(2,1)S(1)} %get-tuple-, ...), kind=kLoop, calls=%fused_computation.226 | loop fusion | bytes 14155776 | tf_op jit(solution)/shard_map/slice | solution.py:51
  132.8 0.8 fusion.13
  133.6 0.8 fusion.21
  135.4 1.4 collective-permute-start.15
  136.8 1.3 collective-permute-start.16
  138.1 3.7 %collective-permute-done.16 = bf16[1,32,384]{2,1,0:T(8,128)(2,1)S(1)} collective-permute-done((bf16[1,32,384]{2,1,0:T(8,128)(2,1)S(1)}, bf16[1,32,384]{2,1,0:T(8,128)(2,1)S(1)}, u32[]{:S(2)}, u32[]{:S(2)}) %collective-permute-start.16) | collective-permute-done | bytes 24608 | tf_op jit(solution)/shard_map/ppermute | solution.py:39
  141.9 3.3 %collective-permute-start.17 = (bf16[18,1,384]{2,1,0:T(2,128)(2,1)S(1)}, bf16[18,1,384]{2,1,0:T(2,128)(2,1)S(1)}, u32[]{:S(2)}, u32[]{:S(2)}) collective-permute-start(bf16[18,1,384]{2,1,0:T(2,128)(2,1)S(1)} %get-tuple-element.48), channel_id=1, source_target_pairs={{0,1},{1,2},{2,3},{4,5},{5,6},{6,7},{8,9},{9,10},{10,11},{12,13},{... | collective-permute-start | bytes 41480 | tf_op jit(solution)/shard_map/ppermute | solution.py:38
  145.2 2.2 %collective-permute-start.18 = (bf16[18,1,384]{2,1,0:T(2,128)(2,1)S(1)}, bf16[18,1,384]{2,1,0:T(2,128)(2,1)S(1)}, u32[]{:S(2)}, u32[]{:S(2)}) collective-permute-start(bf16[18,1,384]{2,1,0:T(2,128)(2,1)S(1)} %get-tuple-element.49), channel_id=1, source_target_pairs={{1,0},{2,1},{3,2},{5,4},{6,5},{7,6},{9,8},{10,9},{11,10},{13,12},{... | collective-permute-start | bytes 41480 | tf_op jit(solution)/shard_map/ppermute | solution.py:39
  147.9 2.5 %collective-permute-done.18 = bf16[18,1,384]{2,1,0:T(2,128)(2,1)S(1)} collective-permute-done((bf16[18,1,384]{2,1,0:T(2,128)(2,1)S(1)}, bf16[18,1,384]{2,1,0:T(2,128)(2,1)S(1)}, u32[]{:S(2)}, u32[]{:S(2)}) %collective-permute-start.18) | collective-permute-done | bytes 13856 | tf_op jit(solution)/shard_map/ppermute | solution.py:39
  150.7 2.3 %broadcast_in_dim.43 = bf16[36,34,2,384]{3,2,1,0:T(2,128)(2,1)} broadcast(bf16[36,34,384]{2,1,0:T(8,128)(2,1)S(1)} %bitcast.209), dimensions={0,1,3} | broadcast | bytes 2820096 | tf_op jit(solution)/shard_map/broadcast_in_dim | solution.py:171
  153.0 4.2 %reshape.476 = bf16[36,68,384]{2,1,0:T(8,128)(2,1)S(1)} reshape(bf16[36,34,2,384]{3,2,1,0:T(2,128)(2,1)} %broadcast_in_dim.43) | data formatting | bytes 3760128 | tf_op jit(solution)/shard_map/reshape | solution.py:171
  157.2 0.9 slice_bitcast_fusion
  158.1 3.6 %fusion.102 = (bf16[1,32,64,384]{3,2,1,0:T(8,128)(2,1)S(1)}, bf16[1,32,64,384]{3,2,1,0:T(8,128)(2,1)S(1)}, bf16[1,32,64,384]{3,2,1,0:T(8,128)(2,1)S(1)}, bf16[1,...) fusion(bf16[1,34,66,384]{3,2,1,0:T(8,128)(2,1)S(1)} %slice_bitc, ...), kind=kLoop, calls=%fused_computation.225 | loop fusion | bytes 28311552 | tf_op jit(solution)/shard_map/slice | solution.py:51
  161.7 0.7 fusion.89
  162.4 0.7 convolution_add_fusion.7
  163.1 0.7 convolution_add_fusion.6
  163.9 0.7 convolution_add_fusion.5
  164.6 0.7 convolution_add_fusion.4
  165.3 0.7 convolution_add_fusion.3
  166.1 0.7 convolution_add_fusion.2
  166.8 0.7 convolution_add_fusion.1
  167.6 0.7 fusion.2
  168.8 2.1 %reshape.478 = bf16[1,32,12288]{2,1,0:T(8,128)(2,1)} reshape(bf16[2048,192]{1,0:T(8,128)(2,1)S(1)} %copy.50) | data formatting | bytes 1572864 | tf_op jit(solution)/shard_map/reshape | solution.py:177
  (189 shorter events, 36.7 us)
Async XLA Ops:
  0.0 101.3 %copy-start = (bf16[432,384]{1,0:T(8,128)(2,1)S(1)}, bf16[432,384]{1,0:T(8,128)(2,1)}, u32[]{:S(2)}) copy-start(bf16[432,384]{1,0:T(8,128)(2,1)} %param.17) | copy-start | bytes 995332
  0.0 12.8 %collective-permute-start = (bf16[1,12416]{1,0:T(2,128)(2,1)}, bf16[1,12416]{1,0:T(2,128)(2,1)S(1)}, u32[]{:S(2)}, u32[]{:S(2)}) collective-permute-start(bf16[1,12416]{1,0:T(2,128)(2,1)} %param.12), channel_id=1, source_target_pairs={{0,1},{1,2},{2,3},{3,4},{4,5},{5,6},{6,7},{7,0},{8,9},{9,10},{10,1... | collective-permute-start | bytes 74504 | tf_op jit(solution)/shard_map/ppermute | solution.py:22
  2.6 12.6 %collective-permute-start.4 = (bf16[1,12416]{1,0:T(2,128)(2,1)}, bf16[1,12416]{1,0:T(2,128)(2,1)S(1)}, u32[]{:S(2)}, u32[]{:S(2)}) collective-permute-start(bf16[1,12416]{1,0:T(2,128)(2,1)} %param.12), channel_id=1, source_target_pairs={{1,0},{2,1},{3,2},{4,3},{5,4},{6,5},{7,6},{0,7},{9,8},{10,9},{11,1... | collective-permute-start | bytes 74504 | tf_op jit(solution)/shard_map/ppermute | solution.py:24
  10.1 11.6 %copy-start.18 = (bf16[1,2,16,512]{3,2,1,0:T(8,128)(2,1)S(1)}, bf16[1,2,16,512]{3,2,1,0:T(8,128)(2,1)}, u32[]{:S(2)}) copy-start(bf16[1,2,16,512]{3,2,1,0:T(8,128)(2,1)} %param.15) | copy-start | bytes 98308
  11.4 12.0 %copy-start.17 = (bf16[1,12416]{1,0:T(2,128)(2,1)S(1)}, bf16[1,12416]{1,0:T(2,128)(2,1)}, u32[]{:S(2)}) copy-start(bf16[1,12416]{1,0:T(2,128)(2,1)} %param.12) | copy-start | bytes 74500
  12.1 47.7 %copy-start.11 = (f32[16,32]{1,0:T(8,128)}, f32[16,32]{1,0:T(8,128)S(1)}, u32[]{:S(2)}) copy-start(f32[16,32]{1,0:T(8,128)S(1)} %get-tuple-element.86) | copy-start | bytes 6148
  12.8 3.0 %collective-permute-start.1 = (bf16[1,12416]{1,0:T(2,128)(2,1)S(1)}, bf16[1,12416]{1,0:T(2,128)(2,1)S(1)}, u32[]{:S(2)}, u32[]{:S(2)}) collective-permute-start(bf16[1,12416]{1,0:T(2,128)(2,1)S(1)} %collective-permute-done), channel_id=1, source_target_pairs={{0,1},{1,2},{2,3},{3,4},{4,5},{5,6},{6,7},{7,0},{8,9},{9,10},{10,1... | collective-permute-start | bytes 74504 | tf_op jit(solution)/shard_map/ppermute | solution.py:22
  15.2 3.6 %collective-permute-start.5 = (bf16[1,12416]{1,0:T(2,128)(2,1)S(1)}, bf16[1,12416]{1,0:T(2,128)(2,1)S(1)}, u32[]{:S(2)}, u32[]{:S(2)}) collective-permute-start(bf16[1,12416]{1,0:T(2,128)(2,1)S(1)} %collective-permute-done.4), channel_id=1, source_target_pairs={{1,0},{2,1},{3,2},{4,3},{5,4},{6,5},{7,6},{0,7},{9,8},{10,9},{11,1... | collective-permute-start | bytes 74504 | tf_op jit(solution)/shard_map/ppermute | solution.py:24
  15.8 3.5 %collective-permute-start.2 = (bf16[1,12416]{1,0:T(2,128)(2,1)S(1)}, bf16[1,12416]{1,0:T(2,128)(2,1)S(1)}, u32[]{:S(2)}, u32[]{:S(2)}) collective-permute-start(bf16[1,12416]{1,0:T(2,128)(2,1)S(1)} %collective-permute-done.1), channel_id=1, source_target_pairs={{0,1},{1,2},{2,3},{3,4},{4,5},{5,6},{6,7},{7,0},{8,9},{9,10},{10,1... | collective-permute-start | bytes 74504 | tf_op jit(solution)/shard_map/ppermute | solution.py:22
  18.8 3.8 %collective-permute-start.6 = (bf16[1,12416]{1,0:T(2,128)(2,1)S(1)}, bf16[1,12416]{1,0:T(2,128)(2,1)S(1)}, u32[]{:S(2)}, u32[]{:S(2)}) collective-permute-start(bf16[1,12416]{1,0:T(2,128)(2,1)S(1)} %collective-permute-done.5), channel_id=1, source_target_pairs={{1,0},{2,1},{3,2},{4,3},{5,4},{6,5},{7,6},{0,7},{9,8},{10,9},{11,1... | collective-permute-start | bytes 74504 | tf_op jit(solution)/shard_map/ppermute | solution.py:24
  19.3 4.0 %collective-permute-start.3 = (bf16[1,12416]{1,0:T(2,128)(2,1)S(1)}, bf16[1,12416]{1,0:T(2,128)(2,1)S(1)}, u32[]{:S(2)}, u32[]{:S(2)}) collective-permute-start(bf16[1,12416]{1,0:T(2,128)(2,1)S(1)} %collective-permute-done.2), channel_id=1, source_target_pairs={{0,1},{1,2},{2,3},{3,4},{4,5},{5,6},{6,7},{7,0},{8,9},{9,10},{10,1... | collective-permute-start | bytes 74504 | tf_op jit(solution)/shard_map/ppermute | solution.py:22
  53.1 6.8 %collective-permute-start.7 = (bf16[3,1,32,16]{3,2,1,0:T(8,128)(2,1)S(1)}, bf16[3,1,32,16]{3,2,1,0:T(8,128)(2,1)S(1)}, u32[]{:S(2)}, u32[]{:S(2)}) collective-permute-start(bf16[3,1,32,16]{3,2,1,0:T(8,128)(2,1)S(1)} %get-tuple-element.84), channel_id=1, source_target_pairs={{0,4},{1,5},{2,6},{3,7},{8,12},{9,13},{10,14},{11,15},{16,20},{17,... | collective-permute-start | bytes 9224 | tf_op jit(solution)/shard_map/ppermute | solution.py:38
  57.2 4.6 %collective-permute-start.8 = (bf16[3,1,32,16]{3,2,1,0:T(8,128)(2,1)S(1)}, bf16[3,1,32,16]{3,2,1,0:T(8,128)(2,1)S(1)}, u32[]{:S(2)}, u32[]{:S(2)}) collective-permute-start(bf16[3,1,32,16]{3,2,1,0:T(8,128)(2,1)S(1)} %get-tuple-element.85), channel_id=1, source_target_pairs={{4,0},{5,1},{6,2},{7,3},{12,8},{13,9},{14,10},{15,11},{20,16},{21,... | collective-permute-start | bytes 9224 | tf_op jit(solution)/shard_map/ppermute | solution.py:39
  61.7 0.8 copy-start.10
  62.5 16.2 %collective-permute-start.10 = (bf16[3,18,1,16]{3,2,1,0:T(2,128)(2,1)}, bf16[3,18,1,16]{3,2,1,0:T(2,128)(2,1)}, u32[]{:S(2)}, u32[]{:S(2)}) collective-permute-start(bf16[3,18,1,16]{3,2,1,0:T(2,128)(2,1)} %get-tuple-element.68), channel_id=1, source_target_pairs={{1,0},{2,1},{3,2},{5,4},{6,5},{7,6},{9,8},{10,9},{11,10},{13,12},{... | collective-permute-start | bytes 5192 | tf_op jit(solution)/shard_map/ppermute | solution.py:39
  72.9 8.1 %collective-permute-start.9 = (bf16[3,18,1,16]{3,2,1,0:T(2,128)(2,1)}, bf16[3,18,1,16]{3,2,1,0:T(2,128)(2,1)}, u32[]{:S(2)}, u32[]{:S(2)}) collective-permute-start(bf16[3,18,1,16]{3,2,1,0:T(2,128)(2,1)} %get-tuple-element.69), channel_id=1, source_target_pairs={{0,1},{1,2},{2,3},{4,5},{5,6},{6,7},{8,9},{9,10},{10,11},{12,13},{... | collective-permute-start | bytes 5192 | tf_op jit(solution)/shard_map/ppermute | solution.py:38
  83.3 2.2 %copy-start.15 = (bf16[512,16]{0,1:T(8,128)(2,1)S(1)}, bf16[512,16]{0,1:T(8,128)(2,1)}, u32[]{:S(2)}) copy-start(bf16[512,16]{0,1:T(8,128)(2,1)} %copy.41) | copy-start | bytes 49156
  83.3 2.8 %copy-start.16 = (bf16[512,16]{0,1:T(8,128)(2,1)S(1)}, bf16[512,16]{0,1:T(8,128)(2,1)}, u32[]{:S(2)}) copy-start(bf16[512,16]{0,1:T(8,128)(2,1)} %concatenate.149) | copy-start | bytes 49156
  83.4 3.9 %copy-start.14 = (bf16[512,16]{0,1:T(8,128)(2,1)S(1)}, bf16[512,16]{0,1:T(8,128)(2,1)}, u32[]{:S(2)}) copy-start(bf16[512,16]{0,1:T(8,128)(2,1)} %copy.42) | copy-start | bytes 49156
  83.4 5.7 %copy-start.13 = (bf16[512,16]{0,1:T(8,128)(2,1)S(1)}, bf16[512,16]{0,1:T(8,128)(2,1)}, u32[]{:S(2)}) copy-start(bf16[512,16]{0,1:T(8,128)(2,1)} %copy.43) | copy-start | bytes 49156
  83.9 17.4 %copy-start.22 = (f32[384]{0:T(512)S(1)}, f32[384]{0:T(512)}, u32[]{:S(2)}) copy-start(f32[384]{0:T(512)} %param.18) | copy-start | bytes 4612
  85.2 17.8 %copy-start.19 = (f32[384]{0:T(512)S(1)}, f32[384]{0:T(512)}, u32[]{:S(2)}) copy-start(f32[384]{0:T(512)} %param.19) | copy-start | bytes 4612
  101.3 17.6 %slice-start = ((s8[7962624]{0:T(1024)(128)(4,1)}), s8[4194304]{0:T(1024)(128)(4,1)S(1)}, s32[]{:S(2)}) async-start(s8[7962624]{0:T(1024)(128)(4,1)} %bitcast.198), calls=%async_computation | async-start | bytes 8388608
  103.4 4.0 %collective-permute-start.11 = (bf16[3,1,32,384]{3,2,1,0:T(8,128)(2,1)S(1)}, bf16[3,1,32,384]{3,2,1,0:T(8,128)(2,1)S(1)}, u32[]{:S(2)}, u32[]{:S(2)}) collective-permute-start(bf16[3,1,32,384]{3,2,1,0:T(8,128)(2,1)S(1)} %get-tuple-element.45), channel_id=1, source_target_pairs={{0,4},{1,5},{2,6},{3,7},{8,12},{9,13},{10,14},{11,15},{16,20},{17,... | collective-permute-start | bytes 221192 | tf_op jit(solution)/shard_map/ppermute | solution.py:38
  104.7 5.1 %collective-permute-start.12 = (bf16[3,1,32,384]{3,2,1,0:T(8,128)(2,1)S(1)}, bf16[3,1,32,384]{3,2,1,0:T(8,128)(2,1)S(1)}, u32[]{:S(2)}, u32[]{:S(2)}) collective-permute-start(bf16[3,1,32,384]{3,2,1,0:T(8,128)(2,1)S(1)} %get-tuple-element.46), channel_id=1, source_target_pairs={{4,0},{5,1},{6,2},{7,3},{12,8},{13,9},{14,10},{15,11},{20,16},{21,... | collective-permute-start | bytes 221192 | tf_op jit(solution)/shard_map/ppermute | solution.py:39
  107.4 11.5 %slice-start.1 = ((s8[7962624]{0:T(1024)(128)(4,1)}), s8[3768320]{0:T(1024)(128)(4,1)S(1)}, s32[]{:S(2)}) async-start(s8[7962624]{0:T(1024)(128)(4,1)} %bitcast.198), calls=%async_computation.1 | async-start | bytes 7536640
  111.7 10.0 %collective-permute-start.13 = (bf16[3,18,1,384]{3,2,1,0:T(2,128)(2,1)S(1)}, bf16[3,18,1,384]{3,2,1,0:T(2,128)(2,1)S(1)}, u32[]{:S(2)}, u32[]{:S(2)}) collective-permute-start(bf16[3,18,1,384]{3,2,1,0:T(2,128)(2,1)S(1)} %get-tuple-element.34), channel_id=1, source_target_pairs={{0,1},{1,2},{2,3},{4,5},{5,6},{6,7},{8,9},{9,10},{10,11},{12,13},{... | collective-permute-start | bytes 124424 | tf_op jit(solution)/shard_map/ppermute | solution.py:38
  113.7 8.0 %collective-permute-start.14 = (bf16[3,18,1,384]{3,2,1,0:T(2,128)(2,1)S(1)}, bf16[3,18,1,384]{3,2,1,0:T(2,128)(2,1)S(1)}, u32[]{:S(2)}, u32[]{:S(2)}) collective-permute-start(bf16[3,18,1,384]{3,2,1,0:T(2,128)(2,1)S(1)} %get-tuple-element.35), channel_id=1, source_target_pairs={{1,0},{2,1},{3,2},{5,4},{6,5},{7,6},{9,8},{10,9},{11,10},{13,12},{... | collective-permute-start | bytes 124424 | tf_op jit(solution)/shard_map/ppermute | solution.py:39
  129.3 1.0 copy-start.8
  129.8 1.0 copy-start.7
  130.2 1.1 copy-start.6
  130.7 1.0 copy-start.5
  131.8 1.0 copy-start.3
  133.5 1.1 copy-start.2
  133.5 1.2 copy-start.4
  133.6 1.2 copy-start.20
  134.8 12.6 %copy-start.12 = (f32[16,32]{1,0:T(8,128)S(1)}, f32[16,32]{1,0:T(8,128)}, u32[]{:S(2)}) copy-start(f32[16,32]{1,0:T(8,128)} %copy-done.11) | copy-start | bytes 6148
  135.4 2.7 %collective-permute-start.15 = (bf16[1,32,384]{2,1,0:T(8,128)(2,1)S(1)}, bf16[1,32,384]{2,1,0:T(8,128)(2,1)S(1)}, u32[]{:S(2)}, u32[]{:S(2)}) collective-permute-start(bf16[1,32,384]{2,1,0:T(8,128)(2,1)S(1)} %get-tuple-element.76), channel_id=1, source_target_pairs={{0,4},{1,5},{2,6},{3,7},{8,12},{9,13},{10,14},{11,15},{16,20},{17,... | collective-permute-start | bytes 73736 | tf_op jit(solution)/shard_map/ppermute | solution.py:38
  136.8 5.0 %collective-permute-start.16 = (bf16[1,32,384]{2,1,0:T(8,128)(2,1)S(1)}, bf16[1,32,384]{2,1,0:T(8,128)(2,1)S(1)}, u32[]{:S(2)}, u32[]{:S(2)}) collective-permute-start(bf16[1,32,384]{2,1,0:T(8,128)(2,1)S(1)} %get-tuple-element.77), channel_id=1, source_target_pairs={{4,0},{5,1},{6,2},{7,3},{12,8},{13,9},{14,10},{15,11},{20,16},{21,... | collective-permute-start | bytes 73736 | tf_op jit(solution)/shard_map/ppermute | solution.py:39
  141.9 6.0 %collective-permute-start.17 = (bf16[18,1,384]{2,1,0:T(2,128)(2,1)S(1)}, bf16[18,1,384]{2,1,0:T(2,128)(2,1)S(1)}, u32[]{:S(2)}, u32[]{:S(2)}) collective-permute-start(bf16[18,1,384]{2,1,0:T(2,128)(2,1)S(1)} %get-tuple-element.48), channel_id=1, source_target_pairs={{0,1},{1,2},{2,3},{4,5},{5,6},{6,7},{8,9},{9,10},{10,11},{12,13},{... | collective-permute-start | bytes 41480 | tf_op jit(solution)/shard_map/ppermute | solution.py:38
  145.2 5.2 %collective-permute-start.18 = (bf16[18,1,384]{2,1,0:T(2,128)(2,1)S(1)}, bf16[18,1,384]{2,1,0:T(2,128)(2,1)S(1)}, u32[]{:S(2)}, u32[]{:S(2)}) collective-permute-start(bf16[18,1,384]{2,1,0:T(2,128)(2,1)S(1)} %get-tuple-element.49), channel_id=1, source_target_pairs={{1,0},{2,1},{3,2},{5,4},{6,5},{7,6},{9,8},{10,9},{11,10},{13,12},{... | collective-permute-start | bytes 41480 | tf_op jit(solution)/shard_map/ppermute | solution.py:39
  158.1 3.6 %copy-start.9 = (bf16[3456,192]{0,1:T(8,128)(2,1)S(1)}, bf16[3456,192]{0,1:T(8,128)(2,1)}, u32[]{:S(2)}) copy-start(bf16[3456,192]{0,1:T(8,128)(2,1)} %param.22) | copy-start | bytes 3981316
  166.8 0.7 copy-start.21
  167.5 3.3 %copy-start.1 = (bf16[432,384]{1,0:T(8,128)(2,1)S(1)}, bf16[432,384]{1,0:T(8,128)(2,1)}, u32[]{:S(2)}) copy-start(bf16[432,384]{1,0:T(8,128)(2,1)} %param.17) | copy-start | bytes 995332
